TPU v7x, 512 devices: a whole 4x4x16 slice. The times are simulated.
512 devices in a mesh: gx: 32 (over y_hi, z), gy: 4 (over x), gz: 4 (over y_lo, core).
Axes of the slice: x: 4, y: 4 (y_hi: 2, y_lo: 2; y = y_hi * 2 + y_lo), z: 16, core: 2. Of those that a mesh axis runs over, the one named last changes fastest.
Arguments:
- fields: float32 [12, 256, 32, 512], P(None, 'gx', 'gy', 'gz'), as said below
- reacting: int32 [256, 32, 512], P('gx', 'gy', 'gz'), may hold values from 0 to 1, as said below
- panel_map: int32 [2, 256, 512], P(None, 'gx', 'gz'), may hold values from 0 to 4095, as said below
- layer_one: bfloat16 [1600, 12], replicated, may hold values from -4 to 4
- layer_two: bfloat16 [800, 1600], replicated, may hold values from -0.21875 to 0.21875
- layer_three: bfloat16 [400, 800], replicated, may hold values from -0.3125 to 0.3125
- layer_four: bfloat16 [12, 400], replicated, may hold values from -0.3125 to 0.3125
Outputs:
- new_fields: float32 [12, 256, 32, 512], P(None, 'gx', 'gy', 'gz')
- impulse: float32 [4096], P(('gx', 'gy', 'gz'))
Inputs may be any that keep to these rules, and one draw needn't show every extreme that they name: `fields`: component 0 (density) lies between 0.3 and 3.3; the velocities (components 1 to 3 over component 0) between -1.2 and 1.2; the pressure 0.4 (component 4 - |momentum|^2 / (2 density)) between 0.3 and 5; components 5 to 11 are 0.01 to 0.14 times component 0. Each device's aligned block of 8 x 8 x 128 cells holds at most 256 reacting cells. The blocks that share their ranges along the second and third dimensions hold exactly 64 reacting cells each on average, and one in eight of them, and at least one, hold exactly 256. `panel_map`: every panel is a patch of 8 x 8 cells of one wall, shifted by 4 cells along the first dimension and closed around it; panels are numbered in a random order and each number is used once.
All inputs are finite; a program needn't handle non-finite values.
Results may differ from a plain program's by a relative error of at most 0.0014.
Values may be sent and summed in bfloat16 or wider, within the bound.
A program may use at most 64 MiB of HBM per device.

v0:
```python
import jax
import jax.numpy as jnp
from jax import lax
from jax.sharding import PartitionSpec as P

BAL = 64
COMPS = 12
PATCH = 8
HEAT_RATIO = 1.4
TIME_STEP = 0.1
CHEM_STEP = 0.25
WENO_EPS = 1e-06


def extended(array, sides, width):
    for axis, dim in sides:
        size, length = (lax.axis_size(axis), array.shape[dim])
        up = [(i, (i + 1) % size) for i in range(size - 1)]
        down = [(j, i) for i, j in up]
        last = lax.slice_in_dim(array, length - width, length, axis=dim)
        initial = lax.slice_in_dim(array, 0, width, axis=dim)
        before = lax.ppermute(last, axis, up)
        after = lax.ppermute(initial, axis, down)
        array = jnp.concatenate([before, array, after], axis=dim)
    return array


def take_slab(array_in, begin_at, length_of, flux_axis):
    return lax.slice_in_dim(array_in, begin_at, begin_at + length_of, axis=flux_axis)


def weno_face(upwind_two, upwind_one, center, downwind_one, downwind_two):
    cand_zero = (2.0 * upwind_two - 7.0 * upwind_one + 11.0 * center) / 6.0
    cand_one = (-upwind_one + 5.0 * center + 2.0 * downwind_one) / 6.0
    cand_two = (2.0 * center + 5.0 * downwind_one - downwind_two) / 6.0
    smooth_zero = (
        13.0 / 12.0 * (upwind_two - 2.0 * upwind_one + center) ** 2
        + 0.25 * (upwind_two - 4.0 * upwind_one + 3.0 * center) ** 2
    )
    smooth_one = (
        13.0 / 12.0 * (upwind_one - 2.0 * center + downwind_one) ** 2
        + 0.25 * (upwind_one - downwind_one) ** 2
    )
    smooth_two = (
        13.0 / 12.0 * (center - 2.0 * downwind_one + downwind_two) ** 2
        + 0.25 * (3.0 * center - 4.0 * downwind_one + downwind_two) ** 2
    )
    weight_zero = 0.1 / (WENO_EPS + smooth_zero) ** 2
    weight_one = 0.6 / (WENO_EPS + smooth_one) ** 2
    weight_two = 0.3 / (WENO_EPS + smooth_two) ** 2
    weight_sum = weight_zero + weight_one + weight_two
    return (weight_zero * cand_zero + weight_one * cand_one + weight_two * cand_two) / weight_sum


def to_recon(fields):
    density = fields[0]
    velocity = fields[1:4] / density[None]
    pressure = (HEAT_RATIO - 1.0) * (
        fields[4] - 0.5 * density * jnp.sum(velocity * velocity, axis=0)
    )
    fractions = fields[5:] / density[None]
    return jnp.concatenate(
        [jnp.log(density)[None], velocity, jnp.log(pressure)[None], fractions], axis=0
    )


def normal_of(normal, ndims):
    return (jnp.arange(3) == normal).reshape((3,) + (1,) * (ndims - 1))


def side_terms(recon, normal):
    density = jnp.exp(recon[0])
    velocity = recon[1:4]
    pressure = jnp.exp(recon[4])
    fractions = recon[5:]
    speed_n = velocity[normal]
    energy = pressure / (HEAT_RATIO - 1.0) + 0.5 * density * jnp.sum(velocity * velocity, axis=0)
    conserved = jnp.concatenate(
        [density[None], density[None] * velocity, energy[None], density[None] * fractions], axis=0
    )
    mass_flux = density * speed_n
    normal_mask = normal_of(normal, recon.ndim)
    momentum_flux = mass_flux[None] * velocity + jnp.where(normal_mask, pressure[None], 0.0)
    flux_terms = jnp.concatenate(
        [
            mass_flux[None],
            momentum_flux,
            ((energy + pressure) * speed_n)[None],
            mass_flux[None] * fractions,
        ],
        axis=0,
    )
    sound_speed = jnp.sqrt(HEAT_RATIO * pressure / density)
    return (
        density,
        velocity,
        pressure,
        fractions,
        energy,
        conserved,
        flux_terms,
        speed_n,
        sound_speed,
    )


def star_state(
    density, velocity, pressure, fractions, energy, speed_n, wave_speed, contact, normal_mask
):
    relative = wave_speed - speed_n
    factor = density * relative / (wave_speed - contact)
    star_velocity = jnp.where(normal_mask, contact[None], velocity)
    star_energy = energy / density + (contact - speed_n) * (
        contact + pressure / (density * relative)
    )
    return jnp.concatenate(
        [
            factor[None],
            factor[None] * star_velocity,
            (factor * star_energy)[None],
            factor[None] * fractions,
        ],
        axis=0,
    )


def hllc_flux(left_recon, right_recon, normal):
    (
        left_density,
        left_velocity,
        left_pressure,
        left_fractions,
        left_energy,
        left_cons,
        left_flux,
        left_speed,
        left_sound,
    ) = side_terms(left_recon, normal)
    (
        right_density,
        right_velocity,
        right_pressure,
        right_fractions,
        right_energy,
        right_cons,
        right_flux,
        right_speed,
        right_sound,
    ) = side_terms(right_recon, normal)
    wave_left = jnp.minimum(left_speed - left_sound, right_speed - right_sound)
    wave_right = jnp.maximum(left_speed + left_sound, right_speed + right_sound)
    left_rel = wave_left - left_speed
    right_rel = wave_right - right_speed
    contact = (
        right_pressure
        - left_pressure
        + left_density * left_speed * left_rel
        - right_density * right_speed * right_rel
    ) / (left_density * left_rel - right_density * right_rel)
    normal_mask = normal_of(normal, left_recon.ndim)
    star_left = star_state(
        left_density,
        left_velocity,
        left_pressure,
        left_fractions,
        left_energy,
        left_speed,
        wave_left,
        contact,
        normal_mask,
    )
    star_right = star_state(
        right_density,
        right_velocity,
        right_pressure,
        right_fractions,
        right_energy,
        right_speed,
        wave_right,
        contact,
        normal_mask,
    )
    left_star_flux = left_flux + wave_left[None] * (star_left - left_cons)
    right_star_flux = right_flux + wave_right[None] * (star_right - right_cons)
    return jnp.where(
        wave_left[None] >= 0,
        left_flux,
        jnp.where(
            contact[None] >= 0,
            left_star_flux,
            jnp.where(wave_right[None] > 0, right_star_flux, right_flux),
        ),
    )


def face_flux(padded, normal):
    flux_axis = normal + 1
    face_count = padded.shape[flux_axis] - 5
    stencil = [take_slab(padded, offset, face_count, flux_axis) for offset in range(6)]
    left_state = weno_face(stencil[0], stencil[1], stencil[2], stencil[3], stencil[4])
    right_state = weno_face(stencil[5], stencil[4], stencil[3], stencil[2], stencil[1])
    return hllc_flux(left_state, right_state, normal)


def mirror_walls(padded, normal, at_first, at_last):
    flux_axis = normal + 1
    cell_count = padded.shape[flux_axis] - 6
    flip_sign = (
        jnp.where(jnp.arange(padded.shape[0]) == 1 + normal, -1.0, 1.0)
        .astype(padded.dtype)
        .reshape((-1, 1, 1, 1))
    )
    ghost_low = jnp.flip(take_slab(padded, 3, 3, flux_axis), flux_axis) * flip_sign
    ghost_high = jnp.flip(take_slab(padded, cell_count, 3, flux_axis), flux_axis) * flip_sign
    low_side = jnp.where(at_first, ghost_low, take_slab(padded, 0, 3, flux_axis))
    high_side = jnp.where(at_last, ghost_high, take_slab(padded, cell_count + 3, 3, flux_axis))
    return jnp.concatenate(
        [low_side, take_slab(padded, 3, cell_count, flux_axis), high_side], axis=flux_axis
    )


def chem_rates(features, layer_one, layer_two, layer_three, layer_four):
    hidden_one = jax.nn.gelu(
        jnp.dot(layer_one, features, preferred_element_type=jnp.float32)
    ).astype(jnp.bfloat16)
    hidden_two = jax.nn.gelu(
        jnp.dot(layer_two, hidden_one, preferred_element_type=jnp.float32)
    ).astype(jnp.bfloat16)
    hidden_three = jax.nn.gelu(
        jnp.dot(layer_three, hidden_two, preferred_element_type=jnp.float32)
    ).astype(jnp.bfloat16)
    return jnp.dot(layer_four, hidden_three, preferred_element_type=jnp.float32).astype(
        jnp.bfloat16
    )


def body(fields, reacting, panel_map, layer_one, layer_two, layer_three, layer_four):
    recon_fields = to_recon(fields)
    gx_count = lax.axis_size("gx")
    gy_count = lax.axis_size("gy")
    gz_count = lax.axis_size("gz")
    at_first = (lax.axis_index("gx") == 0, lax.axis_index("gy") == 0, lax.axis_index("gz") == 0)
    at_last = (
        lax.axis_index("gx") == gx_count - 1,
        lax.axis_index("gy") == gy_count - 1,
        lax.axis_index("gz") == gz_count - 1,
    )
    padded = extended(recon_fields, (("gx", 1), ("gy", 2), ("gz", 3)), 3)
    line_fields = (padded[:, :, 3:-3, 3:-3], padded[:, 3:-3, :, 3:-3], padded[:, 3:-3, 3:-3, :])
    update = jnp.zeros_like(fields)
    push_low = None
    push_high = None
    for normal in range(3):
        line_block = mirror_walls(line_fields[normal], normal, at_first[normal], at_last[normal])
        face_fluxes = face_flux(line_block, normal)
        cell_count = face_fluxes.shape[normal + 1] - 1
        change = take_slab(face_fluxes, 1, cell_count, normal + 1) - take_slab(
            face_fluxes, 0, cell_count, normal + 1
        )
        update = update + change
        if normal == 1:
            push_low = face_fluxes[2, :, 0, :]
            push_high = face_fluxes[2, :, cell_count, :]
    cell_total = reacting.size
    react_flags = reacting.reshape(cell_total)
    capacity = BAL * min(4, gx_count)
    per_peer = capacity // gx_count
    row_rank = jnp.cumsum(react_flags) - 1
    slot_index = jnp.where(
        react_flags == 1, row_rank % gx_count * per_peer + row_rank // gx_count, capacity
    )
    flat_features = recon_fields.reshape(COMPS, cell_total).astype(jnp.bfloat16)
    packed = (
        jnp.zeros((COMPS, capacity), jnp.bfloat16).at[:, slot_index].set(flat_features, mode="drop")
    )
    rate_packed = chem_rates(packed, layer_one, layer_two, layer_three, layer_four)
    gathered = rate_packed[:, jnp.where(react_flags == 1, slot_index, 0)]
    source = jnp.where(react_flags[None, :] == 1, gathered.astype(jnp.float32), 0.0).reshape(
        fields.shape
    )
    new_fields = fields - TIME_STEP * update + CHEM_STEP * source
    on_low = lax.axis_index("gy") == 0
    on_high = lax.axis_index("gy") == gy_count - 1
    push_values = jnp.concatenate(
        [
            jnp.where(on_low, push_low, 0.0).reshape(-1),
            jnp.where(on_high, push_high, 0.0).reshape(-1),
        ]
    )
    panel_ids = jnp.concatenate([panel_map[0].reshape(-1), panel_map[1].reshape(-1)])
    panels_all = 2 * (fields.shape[1] * gx_count // PATCH) * (fields.shape[3] * gz_count // PATCH)
    own_panels = panels_all // (gx_count * gy_count * gz_count)
    partial_loads = jax.ops.segment_sum(push_values, panel_ids, num_segments=panels_all)
    totals = lax.psum(partial_loads, ("gx", "gy", "gz"))
    flat_index = (
        lax.axis_index("gx") * gy_count + lax.axis_index("gy")
    ) * gz_count + lax.axis_index("gz")
    result = lax.dynamic_slice_in_dim(totals, flat_index * own_panels, own_panels)
    impulse = result / float(PATCH * PATCH)
    return (new_fields, impulse)


def solution(mesh):
    return jax.shard_map(
        body,
        mesh=mesh,
        in_specs=(
            P(None, "gx", "gy", "gz"),
            P("gx", "gy", "gz"),
            P(None, "gx", "gz"),
            P(),
            P(),
            P(),
            P(),
        ),
        out_specs=(P(None, "gx", "gy", "gz"), P(("gx", "gy", "gz"))),
        check_vma=False,
    )
```

profile of v0, /device:TPU:1, one launch (start us, length us, event | category | flops | bytes accessed | tf_op | source)
XLA Modules:
  0.0 275.4 jit_solution(14904916895954684997)
XLA Ops:
  5.1 5.0 %collective-permute-start = (f32[12,3,8,128]{3,2,1,0:T(8,128)}, f32[12,3,8,128]{3,2,1,0:T(8,128)}, u32[]{:S(2)}, u32[]{:S(2)}) collective-permute-start(f32[12,3,8,128]{3,2,1,0:T(8,128)} %get-tuple-element.138), channel_id=1, source_target_pairs={{0,16},{16,32},{32,48},{48,64},{64,80},{80,96},{96,112},{112,128},... | collective-permute-start | bytes 442376 | tf_op jit(solution)/shard_map/ppermute | solution.py:22
  10.2 1.3 collective-permute-start.1
  16.4 2.7 copy.63
  21.6 21.7 %scatter_custom_fusion = bf16[12,256]{0,1:T(8,128)(2,1)} fusion(s32[8192]{0:T(1024)S(1)} %bitcast.214, bf16[8192,12]{1,0:T(8,128)(2,1)} %copy.63, bf16[]{:T(256)} %constant.78.clone.1), kind=kCustom, calls=%fused_computation.316 | custom fusion | bytes 6656 | tf_op jit(solution)/shard_map/scatter | solution.py:274
  43.3 3.2 %fusion.16 = bf16[800,256]{1,0:T(8,128)(2,1)} fusion(bf16[800,1600]{1,0:T(8,128)(2,1)S(1)} %copy-done, bf16[12,256]{0,1:T(8,128)(2,1)} %scatter_custom_fusion, bf16[1600,12]{0,1:T(8,128)(2,1)} %param.10), kind=kOutput, calls=%fused_computation.28 | convolution fusion | flops 670720000 | bytes 3014144 | tf_op jit(solution)/shard_map/dot_general | solution.py:227
  46.5 1.8 fusion.8
  48.8 1.8 rev.23
  50.6 1.8 rev.24
  52.4 1.9 rev.25
  55.4 29.4 %gather_fusion = bf16[8192,12]{1,0:T(8,128)(2,1)} fusion(bf16[12,256]{0,1:T(8,128)(2,1)S(1)} %copy.64, s32[8192]{0:T(1024)S(1)} %broadcast_clamp_fusion), kind=kCustom, calls=%fused_computation | custom fusion | bytes 425984 | tf_op jit(solution)/shard_map/gather | solution.py:277
  84.8 3.8 %convert_element_type.31 = f32[8192,12]{1,0:T(8,128)} convert(bf16[8192,12]{1,0:T(8,128)(2,1)} %gather_fusion) | non-fusion elementwise | flops 98304 | bytes 589824 | tf_op jit(solution)/shard_map/convert_element_type | solution.py:278
  88.6 3.6 %copy.66 = f32[12,8,8,128]{3,2,1,0:T(8,128)} copy(f32[12,8,8,128]{0,3,2,1:T(8,128)} %bitcast.175) | data formatting | bytes 786432 | tf_op jit(solution)/shard_map/convert_element_type | solution.py:278
  94.0 1.9 add_divide_fusion.2
  97.2 3.1 %collective-permute-start.2 = (f32[12,14,3,128]{3,1,2,0:T(8,128)S(1)}, f32[12,14,3,128]{3,1,2,0:T(8,128)S(1)}, u32[]{:S(2)}, u32[]{:S(2)}) collective-permute-start(f32[12,14,3,128]{3,1,2,0:T(8,128)S(1)} %copy.53), channel_id=1, source_target_pairs={{0,4},{4,8},{8,12},{1,5},{5,9},{9,13},{2,6},{6,10},{10,14},{3,7},{... | collective-permute-start | bytes 774152 | tf_op jit(solution)/shard_map/ppermute | solution.py:22
  100.4 1.5 collective-permute-start.3
  103.0 1.9 collective-permute-done.2
  105.1 3.7 %collective-permute-done.3 = f32[12,14,3,128]{3,1,2,0:T(8,128)S(1)} collective-permute-done((f32[12,14,3,128]{3,1,2,0:T(8,128)S(1)}, f32[12,14,3,128]{3,1,2,0:T(8,128)S(1)}, u32[]{:S(2)}, u32[]{:S(2)}) %collective-permute-start.3) | collective-permute-done | bytes 258080 | tf_op jit(solution)/shard_map/ppermute | solution.py:23
  109.9 3.6 %add_divide_fusion.1 = (f32[12,8,9,128]{3,2,1,0:T(8,128)S(1)}, f32[12,8,9,128]{3,2,1,0:T(8,128)S(1)}) fusion(f32[12,8,11,128]{3,2,1,0:T(8,128)S(1)} %get-tuple-element.130, f32[12,8,11,128]{3,2,1,0:T(8,128)S(1)} %get-tuple-element.131), kind=kLoop, calls=%fused_computation.80 | loop fusion | flops 13713408 | bytes 3538944 | tf_op jit(solution)/shard_map/div | solution.py:52
  116.2 14.0 %scatter_custom_fusion.1 = f32[4096]{0:T(1024)S(1)} fusion(s32[2048]{0:T(1024)} %pad_add_fusion, f32[2048]{0:T(1024)S(1)} %pad_maximum_fusion.9, f32[]{:T(128)} %constant.54.clone.1), kind=kCustom, calls=%fused_computation.342 | custom fusion | flops 2048 | bytes 16896 | tf_op jit(solution)/shard_map/scatter-add | solution.py:293
  130.3 111.0 %psum.7 = f32[4096]{0:T(1024)S(1)} all-reduce(f32[4096]{0:T(1024)S(1)} %scatter_custom_fusion.1), channel_id=1, replica_groups=mesh['gx'=32,'gy'=4,'gz'=4] {'gx','gy','gz'}, use_global_device_ids=true, to_apply=%region_11.12 | all-reduce | flops 4096 | bytes 32768 | tf_op jit(solution)/shard_map/psum | solution.py:294
  241.3 1.5 pad_maximum_fusion
  242.8 2.0 fusion.169
  244.8 3.4 %copy.59 = f32[12,14,14,3]{2,1,3,0:T(8,128)} copy(f32[12,14,14,3]{3,2,1,0:T(8,128)} %get-tuple-element.58) | data formatting | bytes 56448 | tf_op jit(solution)/shard_map/slice | solution.py:20
  248.2 2.1 collective-permute-start.4
  250.3 3.4 %copy.61 = f32[12,14,14,3]{2,1,3,0:T(8,128)} copy(f32[12,14,14,3]{3,2,1,0:T(8,128)} %get-tuple-element.57) | data formatting | bytes 56448 | tf_op jit(solution)/shard_map/slice | solution.py:21
  253.7 2.9 %collective-permute-start.5 = (f32[12,14,14,3]{2,1,3,0:T(8,128)}, f32[12,14,14,3]{2,1,3,0:T(8,128)}, u32[]{:S(2)}, u32[]{:S(2)}) collective-permute-start(f32[12,14,14,3]{2,1,3,0:T(8,128)} %copy.61), channel_id=1, source_target_pairs={{1,0},{2,1},{3,2},{5,4},{6,5},{7,6},{9,8},{10,9},{11,10},{13,12},{... | collective-permute-start | bytes 84680 | tf_op jit(solution)/shard_map/ppermute | solution.py:23
  257.2 1.7 slice.418
  258.9 2.3 copy.67
  262.1 1.7 slice.424
  263.8 2.3 copy.68
  266.1 1.5 multiply_select_fusion
  267.8 3.9 %add_divide_fusion = (f32[12,8,8,129]{3,2,1,0:T(8,128)S(1)}, f32[12,8,8,129]{3,2,1,0:T(8,128)S(1)}) fusion(f32[12,8,8,131]{3,2,1,0:T(8,128)S(1)} %get-tuple-element.134, f32[12,8,8,131]{3,2,1,0:T(8,128)S(1)} %get-tuple-element.135), kind=kLoop, calls=%fused_computation.53 | loop fusion | flops 12284928 | bytes 3170304 | tf_op jit(solution)/shard_map/div | solution.py:52
  (119 shorter events, 26.8 us)
Async XLA Ops:
  0.6 42.6 %copy-start = (bf16[800,1600]{1,0:T(8,128)(2,1)S(1)}, bf16[800,1600]{1,0:T(8,128)(2,1)}, u32[]{:S(2)}) copy-start(bf16[800,1600]{1,0:T(8,128)(2,1)} %param.11) | copy-start | bytes 7680004
  4.3 11.0 %copy-start.10 = (s32[2,8,128]{2,1,0:T(8,128)S(1)}, s32[2,8,128]{2,1,0:T(8,128)}, u32[]{:S(2)}) copy-start(s32[2,8,128]{2,1,0:T(8,128)} %param.9) | copy-start | bytes 24580
  5.1 87.6 %collective-permute-start = (f32[12,3,8,128]{3,2,1,0:T(8,128)}, f32[12,3,8,128]{3,2,1,0:T(8,128)}, u32[]{:S(2)}, u32[]{:S(2)}) collective-permute-start(f32[12,3,8,128]{3,2,1,0:T(8,128)} %get-tuple-element.138), channel_id=1, source_target_pairs={{0,16},{16,32},{32,48},{48,64},{64,80},{80,96},{96,112},{112,128},... | collective-permute-start | bytes 442376 | tf_op jit(solution)/shard_map/ppermute | solution.py:22
  10.2 82.6 %collective-permute-start.1 = (f32[12,3,8,128]{3,2,1,0:T(8,128)}, f32[12,3,8,128]{3,2,1,0:T(8,128)}, u32[]{:S(2)}, u32[]{:S(2)}) collective-permute-start(f32[12,3,8,128]{3,2,1,0:T(8,128)} %get-tuple-element.139), channel_id=1, source_target_pairs={{16,0},{32,16},{48,32},{64,48},{80,64},{96,80},{112,96},{128,112},... | collective-permute-start | bytes 442376 | tf_op jit(solution)/shard_map/ppermute | solution.py:23
  15.3 3.8 %copy-start.9 = (s32[8,8,128]{2,1,0:T(8,128)S(1)}, s32[8,8,128]{2,1,0:T(8,128)}, u32[]{:S(2)}) copy-start(s32[8,8,128]{2,1,0:T(8,128)} %param.8) | copy-start | bytes 98308
  43.3 3.2 %copy-start.16 = (bf16[12,400]{1,0:T(8,128)(2,1)S(1)}, bf16[12,400]{1,0:T(8,128)(2,1)}, u32[]{:S(2)}) copy-start(bf16[12,400]{1,0:T(8,128)(2,1)} %param.13) | copy-start | bytes 28804
  88.6 4.2 %copy-start.15 = (f32[12]{0:T(128)S(1)}, f32[12]{0:T(128)}, u32[]{:S(2)}) copy-start(f32[12]{0:T(128)} %compare_select_fusion.7) | copy-start | bytes 148
  97.2 7.7 %collective-permute-start.2 = (f32[12,14,3,128]{3,1,2,0:T(8,128)S(1)}, f32[12,14,3,128]{3,1,2,0:T(8,128)S(1)}, u32[]{:S(2)}, u32[]{:S(2)}) collective-permute-start(f32[12,14,3,128]{3,1,2,0:T(8,128)S(1)} %copy.53), channel_id=1, source_target_pairs={{0,4},{4,8},{8,12},{1,5},{5,9},{9,13},{2,6},{6,10},{10,14},{3,7},{... | collective-permute-start | bytes 774152 | tf_op jit(solution)/shard_map/ppermute | solution.py:22
  100.4 8.4 %collective-permute-start.3 = (f32[12,14,3,128]{3,1,2,0:T(8,128)S(1)}, f32[12,14,3,128]{3,1,2,0:T(8,128)S(1)}, u32[]{:S(2)}, u32[]{:S(2)}) collective-permute-start(f32[12,14,3,128]{3,1,2,0:T(8,128)S(1)} %copy.55), channel_id=1, source_target_pairs={{4,0},{8,4},{12,8},{5,1},{9,5},{13,9},{6,2},{10,6},{14,10},{7,3},{... | collective-permute-start | bytes 774152 | tf_op jit(solution)/shard_map/ppermute | solution.py:23
  102.0 0.7 copy-start.14
  102.7 6.2 %copy-start.7 = (f32[12,8,3,128]{3,2,1,0:T(4,128)S(1)}, f32[12,8,3,128]{3,2,1,0:T(4,128)}, u32[]{:S(2)}) copy-start(f32[12,8,3,128]{3,2,1,0:T(4,128)} %rev.23) | copy-start | bytes 442372
  102.7 6.2 %copy-start.8 = (f32[12,8,3,128]{3,2,1,0:T(4,128)S(1)}, f32[12,8,3,128]{3,2,1,0:T(4,128)}, u32[]{:S(2)}) copy-start(f32[12,8,3,128]{3,2,1,0:T(4,128)} %rev.24) | copy-start | bytes 442372
  105.0 4.1 %copy-start.3 = (f32[12,14,3,128]{3,2,1,0:T(4,128)}, f32[12,14,3,128]{3,2,1,0:T(4,128)S(1)}, u32[]{:S(2)}) copy-start(f32[12,14,3,128]{3,2,1,0:T(4,128)S(1)} %copy.54) | copy-start | bytes 774148
  109.0 0.7 copy-start.4
  114.0 0.7 copy-start.13
  115.3 0.9 copy-start.1
  248.2 9.0 %collective-permute-start.4 = (f32[12,14,14,3]{2,1,3,0:T(8,128)}, f32[12,14,14,3]{2,1,3,0:T(8,128)}, u32[]{:S(2)}, u32[]{:S(2)}) collective-permute-start(f32[12,14,14,3]{2,1,3,0:T(8,128)} %copy.59), channel_id=1, source_target_pairs={{0,1},{1,2},{2,3},{4,5},{5,6},{6,7},{8,9},{9,10},{10,11},{12,13},{... | collective-permute-start | bytes 84680 | tf_op jit(solution)/shard_map/ppermute | solution.py:22
  250.3 15.7 %copy-start.12 = (f32[12]{0:T(128)S(1)}, f32[12]{0:T(128)}, u32[]{:S(2)}) copy-start(f32[12]{0:T(128)} %compare_select_fusion.5) | copy-start | bytes 148
  253.7 8.3 %collective-permute-start.5 = (f32[12,14,14,3]{2,1,3,0:T(8,128)}, f32[12,14,14,3]{2,1,3,0:T(8,128)}, u32[]{:S(2)}, u32[]{:S(2)}) collective-permute-start(f32[12,14,14,3]{2,1,3,0:T(8,128)} %copy.61), channel_id=1, source_target_pairs={{1,0},{2,1},{3,2},{5,4},{6,5},{7,6},{9,8},{10,9},{11,10},{13,12},{... | collective-permute-start | bytes 84680 | tf_op jit(solution)/shard_map/ppermute | solution.py:23
  272.3 0.7 copy-start.11
  273.1 1.1 copy-start.2
  273.1 1.2 copy-start.5
  273.1 1.3 copy-start.6
where the time goes:
time: 276 us; the launch traced here: 275 us
  blocking collectives  111 us (40%)
  local copies, waits for them, and re-layouts  87.9 us (32%)
  other arithmetic  47.9 us (17%)
  starting transfers between devices  15.9 us (6%)
  waiting for transfers between devices  6.54 us (2%)
  matrix products  4.97 us (2%)
    psum x1, blocking collectives, body(): totals = lax.psum(partial_loads, ('gx', 'gy', 'gz'))  111 us
    gather x1, local copies, waits for them, and re-layouts, body(): gathered = rate_packed[:, jnp.where(react_flags == 1, slot_index, 0)]  29.4 us
    scatter x1, local copies, waits for them, and re-layouts, body(): jnp.zeros((COMPS, capacity), jnp.bfloat16).at[:, slot_index]  21.7 us
    scatter-add x1, other arithmetic, body(): jax.ops.segment_sum(push_values, panel_ids, num_segments=panels_all)  14 us
    ppermute x3, starting transfers between devices, extended(): before = lax.ppermute(last, axis, up)  10.3 us
    div x3, other arithmetic, weno_face(): (weight_zero * cand_zero + weight_one * cand_one + weight_two * cand_two)...  9.43 us
    unnamed x38, local copies, waits for them, and re-layouts  7.97 us
    ppermute x3, starting transfers between devices, extended(): after = lax.ppermute(initial, axis, down)  5.61 us
  transfers between devices with their start and end apart: 6, of which 3 were waited for; matrix products, arithmetic and copies ran while one was open for 33% of the time, Pallas kernels for 0%

commit v1 on v0

--- a/solution.py
+++ b/solution.py
@@ -2,6 +2,7 @@
 import jax.numpy as jnp
 from jax import lax
 from jax.sharding import PartitionSpec as P
+from jax.lax import psum
 
 BAL = 64
 COMPS = 12
@@ -291,7 +292,8 @@
     panels_all = 2 * (fields.shape[1] * gx_count // PATCH) * (fields.shape[3] * gz_count // PATCH)
     own_panels = panels_all // (gx_count * gy_count * gz_count)
     partial_loads = jax.ops.segment_sum(push_values, panel_ids, num_segments=panels_all)
-    totals = lax.psum(partial_loads, ("gx", "gy", "gz"))
+    part_now = psum(partial_loads, ("gy", "gz"))
+    totals = psum(part_now, "gx")
     flat_index = (
         lax.axis_index("gx") * gy_count + lax.axis_index("gy")
     ) * gz_count + lax.axis_index("gz")

time: 276 us -> 374 us (1.36)
  blocking collectives: 111 us -> 178 us
  starting transfers between devices: 15.9 us -> 47.2 us
    psum x1 -> x2, blocking collectives: 111 us -> 178 us  [the longest x1 127 us: body(): totals = psum(part_now, 'gx')]
    ppermute x3, starting transfers between devices: 10.3 us -> 39.1 us  [extended(): before = lax.ppermute(last, axis, up)]
  transfers between devices with their start and end apart: 6 -> 6, of which waited for: 3 -> 2; matrix products, arithmetic and copies ran while one was open for 33% -> 24% of each run, Pallas kernels for 0% -> 0%
where the time goes in v1:
time: 374 us; the launch traced here: 373 us
  blocking collectives  178 us (48%)
  local copies, waits for them, and re-layouts  87.6 us (23%)
  other arithmetic  47.9 us (13%)
  starting transfers between devices  47.2 us (13%)
  waiting for transfers between devices  5.66 us (2%)
  matrix products  4.96 us (1%)
    psum x1, blocking collectives, body(): totals = psum(part_now, 'gx')  127 us
    psum x1, blocking collectives, body(): part_now = psum(partial_loads, ('gy', 'gz'))  51.3 us
    ppermute x3, starting transfers between devices, extended(): before = lax.ppermute(last, axis, up)  39.1 us
    gather x1, local copies, waits for them, and re-layouts, body(): gathered = rate_packed[:, jnp.where(react_flags == 1, slot_index, 0)]  29.2 us
    scatter x1, local copies, waits for them, and re-layouts, body(): jnp.zeros((COMPS, capacity), jnp.bfloat16).at[:, slot_index]  21.7 us
    scatter-add x1, other arithmetic, body(): jax.ops.segment_sum(push_values, panel_ids, num_segments=panels_all)  14 us
    div x3, other arithmetic, weno_face(): (weight_zero * cand_zero + weight_one * cand_one + weight_two * cand_two)...  9.43 us
    ppermute x3, starting transfers between devices, extended(): after = lax.ppermute(initial, axis, down)  8.07 us
  transfers between devices with their start and end apart: 6, of which 2 were waited for; matrix products, arithmetic and copies ran while one was open for 24% of the time, Pallas kernels for 0%

profile of v1, /device:TPU:1, one launch (start us, length us, event | category | flops | bytes accessed | tf_op | source)
XLA Modules:
  0.0 372.8 jit_solution(12230809834034627826)
XLA Ops:
  5.1 5.0 %collective-permute-start = (f32[12,3,8,128]{3,2,1,0:T(8,128)}, f32[12,3,8,128]{3,2,1,0:T(8,128)}, u32[]{:S(2)}, u32[]{:S(2)}) collective-permute-start(f32[12,3,8,128]{3,2,1,0:T(8,128)} %get-tuple-element.138), channel_id=1, source_target_pairs={{0,16},{16,32},{32,48},{48,64},{64,80},{80,96},{96,112},{112,128},... | collective-permute-start | bytes 442376 | tf_op jit(solution)/shard_map/ppermute | solution.py:23
  16.5 2.7 copy.63
  21.6 21.7 %scatter_custom_fusion = bf16[12,256]{0,1:T(8,128)(2,1)} fusion(s32[8192]{0:T(1024)S(1)} %bitcast.214, bf16[8192,12]{1,0:T(8,128)(2,1)} %copy.63, bf16[]{:T(256)} %constant.78.clone.1), kind=kCustom, calls=%fused_computation.316 | custom fusion | bytes 6656 | tf_op jit(solution)/shard_map/scatter | solution.py:275
  43.3 3.2 fusion.16
  46.5 1.8 fusion.8
  48.8 1.8 rev.23
  50.6 1.8 rev.24
  52.4 1.9 rev.25
  55.4 29.2 %gather_fusion = bf16[8192,12]{1,0:T(8,128)(2,1)} fusion(bf16[12,256]{0,1:T(8,128)(2,1)S(1)} %copy.64, s32[8192]{0:T(1024)S(1)} %broadcast_clamp_fusion), kind=kCustom, calls=%fused_computation | custom fusion | bytes 425984 | tf_op jit(solution)/shard_map/gather | solution.py:278
  84.6 3.8 %convert_element_type.31 = f32[8192,12]{1,0:T(8,128)} convert(bf16[8192,12]{1,0:T(8,128)(2,1)} %gather_fusion) | non-fusion elementwise | flops 98304 | bytes 589824 | tf_op jit(solution)/shard_map/convert_element_type | solution.py:279
  88.4 3.6 copy.66
  93.8 1.9 add_divide_fusion.2
  97.0 3.1 collective-permute-start.2
  100.2 1.5 collective-permute-start.3
  102.8 1.9 collective-permute-done.2
  104.9 3.7 %collective-permute-done.3 = f32[12,14,3,128]{3,1,2,0:T(8,128)S(1)} collective-permute-done((f32[12,14,3,128]{3,1,2,0:T(8,128)S(1)}, f32[12,14,3,128]{3,1,2,0:T(8,128)S(1)}, u32[]{:S(2)}, u32[]{:S(2)}) %collective-permute-start.3) | collective-permute-done | bytes 258080 | tf_op jit(solution)/shard_map/ppermute | solution.py:24
  109.7 3.6 add_divide_fusion.1
  116.0 14.0 %scatter_custom_fusion.1 = f32[4096]{0:T(1024)S(1)} fusion(s32[2048]{0:T(1024)} %pad_add_fusion, f32[2048]{0:T(1024)S(1)} %pad_maximum_fusion.9, f32[]{:T(128)} %constant.54.clone.1), kind=kCustom, calls=%fused_computation.342 | custom fusion | flops 2048 | bytes 16896 | tf_op jit(solution)/shard_map/scatter-add | solution.py:294
  130.1 51.3 %psum.14 = f32[4096]{0:T(1024)S(1)} all-reduce(f32[4096]{0:T(1024)S(1)} %scatter_custom_fusion.1), channel_id=1, replica_groups=mesh['gx'=32,'gy'=4,'gz'=4] {'gy','gz'}, use_global_device_ids=true, to_apply=%region_11.12 | all-reduce | flops 4096 | bytes 32768 | tf_op jit(solution)/shard_map/psum | solution.py:295
  181.4 127.0 %psum.15 = f32[4096]{0:T(1024)S(1)} all-reduce(f32[4096]{0:T(1024)S(1)} %psum.14), channel_id=1, replica_groups=mesh['gx'=32,'gy'=4,'gz'=4] {'gx'}, use_global_device_ids=true, to_apply=%region_12.13 | all-reduce | flops 4096 | bytes 32768 | tf_op jit(solution)/shard_map/psum | solution.py:296
  308.3 1.5 pad_maximum_fusion
  309.8 2.0 fusion.169
  311.8 3.4 copy.59
  315.2 30.9 %collective-permute-start.4 = (f32[12,14,14,3]{2,1,3,0:T(8,128)}, f32[12,14,14,3]{2,1,3,0:T(8,128)}, u32[]{:S(2)}, u32[]{:S(2)}) collective-permute-start(f32[12,14,14,3]{2,1,3,0:T(8,128)} %copy.59), channel_id=1, source_target_pairs={{0,1},{1,2},{2,3},{4,5},{5,6},{6,7},{8,9},{9,10},{10,11},{12,13},{... | collective-permute-start | bytes 84680 | tf_op jit(solution)/shard_map/ppermute | solution.py:23
  346.2 3.4 copy.61
  349.5 5.3 %collective-permute-start.5 = (f32[12,14,14,3]{2,1,3,0:T(8,128)}, f32[12,14,14,3]{2,1,3,0:T(8,128)}, u32[]{:S(2)}, u32[]{:S(2)}) collective-permute-start(f32[12,14,14,3]{2,1,3,0:T(8,128)} %copy.61), channel_id=1, source_target_pairs={{1,0},{2,1},{3,2},{5,4},{6,5},{7,6},{9,8},{10,9},{11,10},{13,12},{... | collective-permute-start | bytes 84680 | tf_op jit(solution)/shard_map/ppermute | solution.py:24
  355.5 1.7 slice.418
  357.2 2.3 copy.67
  359.5 1.7 slice.424
  361.2 2.3 copy.68
  363.5 1.5 multiply_select_fusion
  365.3 3.9 %add_divide_fusion = (f32[12,8,8,129]{3,2,1,0:T(8,128)S(1)}, f32[12,8,8,129]{3,2,1,0:T(8,128)S(1)}) fusion(f32[12,8,8,131]{3,2,1,0:T(8,128)S(1)} %get-tuple-element.134, f32[12,8,8,131]{3,2,1,0:T(8,128)S(1)} %get-tuple-element.135), kind=kLoop, calls=%fused_computation.53 | loop fusion | flops 12284928 | bytes 3170304 | tf_op jit(solution)/shard_map/div | solution.py:53
  (120 shorter events, 27.2 us)
Async XLA Ops:
  0.6 42.7 %copy-start = (bf16[800,1600]{1,0:T(8,128)(2,1)S(1)}, bf16[800,1600]{1,0:T(8,128)(2,1)}, u32[]{:S(2)}) copy-start(bf16[800,1600]{1,0:T(8,128)(2,1)} %param.11) | copy-start | bytes 7680004
  4.3 11.0 %copy-start.10 = (s32[2,8,128]{2,1,0:T(8,128)S(1)}, s32[2,8,128]{2,1,0:T(8,128)}, u32[]{:S(2)}) copy-start(s32[2,8,128]{2,1,0:T(8,128)} %param.9) | copy-start | bytes 24580
  5.1 87.4 %collective-permute-start = (f32[12,3,8,128]{3,2,1,0:T(8,128)}, f32[12,3,8,128]{3,2,1,0:T(8,128)}, u32[]{:S(2)}, u32[]{:S(2)}) collective-permute-start(f32[12,3,8,128]{3,2,1,0:T(8,128)} %get-tuple-element.138), channel_id=1, source_target_pairs={{0,16},{16,32},{32,48},{48,64},{64,80},{80,96},{96,112},{112,128},... | collective-permute-start | bytes 442376 | tf_op jit(solution)/shard_map/ppermute | solution.py:23
  10.2 82.4 %collective-permute-start.1 = (f32[12,3,8,128]{3,2,1,0:T(8,128)}, f32[12,3,8,128]{3,2,1,0:T(8,128)}, u32[]{:S(2)}, u32[]{:S(2)}) collective-permute-start(f32[12,3,8,128]{3,2,1,0:T(8,128)} %get-tuple-element.139), channel_id=1, source_target_pairs={{16,0},{32,16},{48,32},{64,48},{80,64},{96,80},{112,96},{128,112},... | collective-permute-start | bytes 442376 | tf_op jit(solution)/shard_map/ppermute | solution.py:24
  15.4 3.8 %copy-start.9 = (s32[8,8,128]{2,1,0:T(8,128)S(1)}, s32[8,8,128]{2,1,0:T(8,128)}, u32[]{:S(2)}) copy-start(s32[8,8,128]{2,1,0:T(8,128)} %param.8) | copy-start | bytes 98308
  43.3 3.2 copy-start.16
  88.4 4.2 %copy-start.15 = (f32[12]{0:T(128)S(1)}, f32[12]{0:T(128)}, u32[]{:S(2)}) copy-start(f32[12]{0:T(128)} %compare_select_fusion.7) | copy-start | bytes 148
  97.0 7.7 %collective-permute-start.2 = (f32[12,14,3,128]{3,1,2,0:T(8,128)S(1)}, f32[12,14,3,128]{3,1,2,0:T(8,128)S(1)}, u32[]{:S(2)}, u32[]{:S(2)}) collective-permute-start(f32[12,14,3,128]{3,1,2,0:T(8,128)S(1)} %copy.53), channel_id=1, source_target_pairs={{0,4},{4,8},{8,12},{1,5},{5,9},{9,13},{2,6},{6,10},{10,14},{3,7},{... | collective-permute-start | bytes 774152 | tf_op jit(solution)/shard_map/ppermute | solution.py:23
  100.2 8.4 %collective-permute-start.3 = (f32[12,14,3,128]{3,1,2,0:T(8,128)S(1)}, f32[12,14,3,128]{3,1,2,0:T(8,128)S(1)}, u32[]{:S(2)}, u32[]{:S(2)}) collective-permute-start(f32[12,14,3,128]{3,1,2,0:T(8,128)S(1)} %copy.55), channel_id=1, source_target_pairs={{4,0},{8,4},{12,8},{5,1},{9,5},{13,9},{6,2},{10,6},{14,10},{7,3},{... | collective-permute-start | bytes 774152 | tf_op jit(solution)/shard_map/ppermute | solution.py:24
  101.8 0.7 copy-start.14
  102.5 6.2 %copy-start.7 = (f32[12,8,3,128]{3,2,1,0:T(4,128)S(1)}, f32[12,8,3,128]{3,2,1,0:T(4,128)}, u32[]{:S(2)}) copy-start(f32[12,8,3,128]{3,2,1,0:T(4,128)} %rev.23) | copy-start | bytes 442372
  102.5 6.2 %copy-start.8 = (f32[12,8,3,128]{3,2,1,0:T(4,128)S(1)}, f32[12,8,3,128]{3,2,1,0:T(4,128)}, u32[]{:S(2)}) copy-start(f32[12,8,3,128]{3,2,1,0:T(4,128)} %rev.24) | copy-start | bytes 442372
  104.8 4.1 %copy-start.3 = (f32[12,14,3,128]{3,2,1,0:T(4,128)}, f32[12,14,3,128]{3,2,1,0:T(4,128)S(1)}, u32[]{:S(2)}) copy-start(f32[12,14,3,128]{3,2,1,0:T(4,128)S(1)} %copy.54) | copy-start | bytes 774148
  108.8 0.7 copy-start.4
  113.8 0.7 copy-start.13
  115.1 0.9 copy-start.1
  315.2 40.3 %collective-permute-start.4 = (f32[12,14,14,3]{2,1,3,0:T(8,128)}, f32[12,14,14,3]{2,1,3,0:T(8,128)}, u32[]{:S(2)}, u32[]{:S(2)}) collective-permute-start(f32[12,14,14,3]{2,1,3,0:T(8,128)} %copy.59), channel_id=1, source_target_pairs={{0,1},{1,2},{2,3},{4,5},{5,6},{6,7},{8,9},{9,10},{10,11},{12,13},{... | collective-permute-start | bytes 84680 | tf_op jit(solution)/shard_map/ppermute | solution.py:23
  346.1 17.3 %copy-start.12 = (f32[12]{0:T(128)S(1)}, f32[12]{0:T(128)}, u32[]{:S(2)}) copy-start(f32[12]{0:T(128)} %compare_select_fusion.5) | copy-start | bytes 148
  349.5 9.9 %collective-permute-start.5 = (f32[12,14,14,3]{2,1,3,0:T(8,128)}, f32[12,14,14,3]{2,1,3,0:T(8,128)}, u32[]{:S(2)}, u32[]{:S(2)}) collective-permute-start(f32[12,14,14,3]{2,1,3,0:T(8,128)} %copy.61), channel_id=1, source_target_pairs={{1,0},{2,1},{3,2},{5,4},{6,5},{7,6},{9,8},{10,9},{11,10},{13,12},{... | collective-permute-start | bytes 84680 | tf_op jit(solution)/shard_map/ppermute | solution.py:24
  369.7 0.6 copy-start.11
  370.5 1.1 copy-start.2
  370.5 1.2 copy-start.5
  370.5 1.3 copy-start.6
